TPU v7x, 32 devices: a whole 2x2x4 slice. The times are simulated.
32 devices in a mesh: req: 8 (over y, x, core), mlp: 4 (over z).
Axes of the slice: x: 2, y: 2, z: 4, core: 2. Of those that a mesh axis runs over, the one named last changes fastest.
Arguments:
- hidden_in: bfloat16 [16, 512, 2048], P('req'), may hold values from -6 to 6
- lengths: int32 [16], replicated, may hold values from 1 to 512, 4096 in all
- slot_request: int32 [16], replicated, may hold values from 0 to 15, each once
- adapter_of: int32 [16], replicated, may hold values from 0 to 63, as said below
- adapter_slot: int32 [64], replicated, may hold values from 0 to 63, each once
- norm_gain_attn: float32 [2048], replicated, may hold values from 0.5 to 1.5
- norm_gain_mlp: float32 [2048], replicated, may hold values from 0.5 to 1.5
- final_gain: float32 [2048], replicated, may hold values from 0.5 to 1.5
- w_qkv: bfloat16 [2048, 3, 2048], P(None, None, 'mlp')
- w_out: bfloat16 [2048, 2048], P('mlp'), may hold values from -0.125 to 0.125
- w_gateup: bfloat16 [2048, 2, 4096], P('req', None, 'mlp'), may hold values from -0.125 to 0.125
- w_down: bfloat16 [4096, 2048], P('mlp', 'req'), may hold values from -0.09375 to 0.09375
- adapter_down: bfloat16 [64, 16, 2048], P('req'), may hold values from -0.125 to 0.125
- adapter_up: bfloat16 [64, 16, 2048], P('req', None, 'mlp'), may hold values from -1.5 to 1.5
- vocab: bfloat16 [49152, 2048], P(('req', 'mlp')), may hold values from -0.375 to 0.375
Outputs:
- out_hidden: bfloat16 [16, 512, 2048], P('req')
- request_norm: float32 [16], replicated
- request_peak: float32 [16], replicated
Inputs may be any that keep to these rules, and one draw needn't show every extreme that they name: Some request has exactly 512 tokens, and all lengths together sum to 4096. `slot_request`: each request sits in exactly one slot. `adapter_of`: exactly 16 distinct adapters are named. `adapter_slot`: each adapter sits in exactly one row of the adapter tables.
All inputs are finite; a program needn't handle non-finite values.
Results may differ from a plain program's by a relative error of at most 0.018.
Values may be sent and summed in bfloat16 or wider, within the bound.
No kernel may reach another device: no remote copies, remote signals or barrier semaphores. Data moves between devices by JAX's collectives and lax.ppermute only.
A program may use at most 128 MiB of HBM per device.

v0:
```python
import jax
import jax.numpy as jnp
from jax import lax
from jax.sharding import PartitionSpec as P

HEAD_WIDTH = 64


EPSILON = 1e-05
ROPE_BASE = 130000.0
ADAPTER_SCALE = 2.0
MASKED = -1e30


def rms_norm(values, gain):
    return values * lax.rsqrt(jnp.mean(values * values, axis=-1, keepdims=True) + EPSILON) * gain


def rotary_embedded(tensor):
    length = tensor.shape[-3]
    half_width = tensor.shape[-1] // 2
    frequency = ROPE_BASE ** (-(jnp.arange(half_width, dtype=jnp.float32) * 2.0 / tensor.shape[-1]))
    angles = jnp.arange(length, dtype=jnp.float32)[:, None] * frequency[None, :]
    cosine = jnp.cos(angles)[:, None, :]
    sine_part = jnp.sin(angles)[:, None, :]
    front_half = tensor[..., :half_width]
    back_half = tensor[..., half_width:]
    return jnp.concatenate(
        [front_half * cosine - back_half * sine_part, back_half * cosine + front_half * sine_part],
        axis=-1,
    )


def per_device(
    hidden_in,
    lengths,
    slot_request,
    adapter_of,
    adapter_slot,
    norm_gain_attn,
    norm_gain_mlp,
    final_gain,
    w_qkv,
    w_out,
    w_gateup,
    w_down,
    adapter_down,
    adapter_up,
    vocab,
):
    req_index = lax.axis_index("req")
    slots_number, sequence_length, width = hidden_in.shape
    row_count = slots_number * sequence_length
    head_cols = w_qkv.shape[2]
    heads_number = head_cols // HEAD_WIDTH
    unit_cols = w_gateup.shape[2]
    requests = lax.dynamic_slice_in_dim(slot_request, req_index * slots_number, slots_number)
    own_lengths = jnp.take(lengths, requests)
    own_adapters = jnp.take(adapter_of, requests)
    table_rows = jnp.take(adapter_slot, own_adapters)
    positions = jnp.arange(sequence_length, dtype=jnp.int32)
    residual_in = hidden_in.astype(jnp.float32)
    normed = rms_norm(residual_in, norm_gain_attn).astype(jnp.bfloat16)
    projected_rows = jnp.dot(
        normed.reshape(row_count, width),
        w_qkv.reshape(width, 3 * head_cols),
        preferred_element_type=jnp.float32,
    ).reshape(slots_number, sequence_length, 3, head_cols)
    down_all, up_all = (
        lax.all_gather(adapter_down, "req", axis=0, tiled=True),
        lax.all_gather(adapter_up, "req", axis=0, tiled=True),
    )
    down_rows = jnp.take(down_all, table_rows, axis=0)
    up_rows = jnp.take(up_all, table_rows, axis=0)
    low_rank = jnp.einsum(
        "bsd,brd->bsr", normed, down_rows, preferred_element_type=jnp.float32
    ).astype(jnp.bfloat16)
    raised_rows = jnp.einsum("bsr,brc->bsc", low_rank, up_rows, preferred_element_type=jnp.float32)
    queries = rotary_embedded(
        (projected_rows[:, :, 0] + ADAPTER_SCALE * raised_rows).reshape(
            slots_number, sequence_length, heads_number, HEAD_WIDTH
        )
    ).astype(jnp.bfloat16)
    key_heads = rotary_embedded(
        projected_rows[:, :, 1].reshape(slots_number, sequence_length, heads_number, HEAD_WIDTH)
    ).astype(jnp.bfloat16)
    value_heads = (
        projected_rows[:, :, 2]
        .reshape(slots_number, sequence_length, heads_number, HEAD_WIDTH)
        .astype(jnp.bfloat16)
    )
    causal = positions[None, :] <= positions[:, None]

    def attend(slot_items):
        query_one, key_one, value_one, length = slot_items
        scores = jnp.einsum(
            "qhd,khd->hqk", query_one, key_one, preferred_element_type=jnp.float32
        ) * HEAD_WIDTH ** (-0.5)
        allowed = causal & (positions[None, :] < length)
        scores = jnp.where(allowed[None], scores, MASKED)
        probabilities = jax.nn.softmax(scores, axis=-1).astype(jnp.bfloat16)
        return jnp.einsum(
            "hqk,khd->qhd", probabilities, value_one, preferred_element_type=jnp.float32
        ).astype(jnp.bfloat16)

    attended = lax.map(attend, (queries, key_heads, value_heads, own_lengths))
    head_part = jnp.dot(
        attended.reshape(row_count, head_cols), w_out, preferred_element_type=jnp.float32
    )
    mixed_heads = lax.psum(head_part.astype(jnp.bfloat16), "mlp").astype(jnp.float32)
    stream = (residual_in + mixed_heads.reshape(slots_number, sequence_length, width)).astype(
        jnp.bfloat16
    )
    normed_mid = (
        rms_norm(stream.astype(jnp.float32), norm_gain_mlp)
        .astype(jnp.bfloat16)
        .reshape(row_count, width)
    )
    shard_piece = lax.all_gather(w_gateup, "req", axis=0, tiled=True)
    gate_up = jnp.dot(
        normed_mid,
        shard_piece.reshape(shard_piece.shape[0], 2 * unit_cols),
        preferred_element_type=jnp.float32,
    )
    activated = (jax.nn.silu(gate_up[:, :unit_cols]) * gate_up[:, unit_cols:]).astype(jnp.bfloat16)
    unit_part = jnp.dot(
        activated,
        lax.all_gather(w_down, "req", axis=1, tiled=True),
        preferred_element_type=jnp.float32,
    )
    unit_total = lax.psum(unit_part.astype(jnp.bfloat16), "mlp").astype(jnp.float32)
    result = stream.astype(jnp.float32) + unit_total.reshape(slots_number, sequence_length, width)
    live = positions[None, :] < own_lengths[:, None]
    out_hidden = jnp.where(live[:, :, None], result, 0.0).astype(jnp.bfloat16)
    out_float = out_hidden.astype(jnp.float32)
    square_sum = jnp.sum(out_float * out_float, axis=(1, 2))
    slot_norm = jnp.sqrt(square_sum / (own_lengths.astype(jnp.float32) * width))
    picked = (positions[None, :] == own_lengths[:, None] - 1).astype(jnp.float32)
    last_rows = jnp.einsum("bs,bsd->bd", picked, out_float, precision=lax.Precision.HIGHEST)
    last_rounded = lax.optimization_barrier(rms_norm(last_rows, final_gain).astype(jnp.bfloat16))
    last_normed = last_rounded.astype(jnp.float32)
    every_last, every_norm = (
        lax.all_gather(last_normed, "req", axis=0, tiled=True),
        lax.all_gather(slot_norm, "req", axis=0, tiled=True),
    )
    logits = lax.dot_general(
        every_last.astype(jnp.bfloat16),
        vocab,
        (((1,), (1,)), ((), ())),
        preferred_element_type=jnp.float32,
    )
    slot_peak = lax.pmax(jnp.max(logits, axis=1), ("req", "mlp"))
    request_total = slot_request.shape[0]
    owners = slot_request[None, :] == jnp.arange(request_total, dtype=jnp.int32)[:, None]
    request_norm = jnp.sum(jnp.where(owners, every_norm[None, :], 0.0), axis=1)
    request_peak = jnp.sum(jnp.where(owners, slot_peak[None, :], 0.0), axis=1)
    return (out_hidden, request_norm, request_peak)


def solution(mesh):
    return jax.shard_map(
        per_device,
        mesh=mesh,
        in_specs=(
            P("req", None, None),
            P(),
            P(),
            P(),
            P(),
            P(),
            P(),
            P(),
            P(None, None, "mlp"),
            P("mlp", None),
            P("req", None, "mlp"),
            P("mlp", "req"),
            P("req", None, None),
            P("req", None, "mlp"),
            P(("req", "mlp"), None),
        ),
        out_specs=(P("req", None, None), P(), P()),
        check_vma=False,
    )
```

profile of v0, /device:TPU:0, one launch (start us, length us, event | category | flops | bytes accessed | tf_op | source)
XLA Modules:
  0.0 621.2 jit_solution(16187059862389544610)
XLA Ops:
  7.2 0.7 all-gather.8.cloned.1.call-update
  8.0 0.7 all-gather.6.cloned.1.call-update
  8.7 8.8 %copy.26 = bf16[2048,3,512]{0,2,1:T(8,128)(2,1)} copy(bf16[2048,3,512]{2,0,1:T(8,128)(2,1)} %param.27) | data formatting | bytes 12582912 | tf_op args[8]
  17.5 3.3 fusion.44
  21.1 9.0 %fusion.53 = f32[2,512,3,512]{1,3,2,0:T(8,128)S(1)} fusion(bf16[2048,3,512]{0,2,1:T(8,128)(2,1)} %copy.26, bf16[2,512,2048]{2,1,0:T(8,128)(2,1)S(1)} %copy-done.4, f32[2048]{0:T(1024)S(1)} %copy-done.13, f32[2,512]{1,0:T(2,128)S(1)} %add_rsqrt_fusion.1), kind=kOutput, calls=%fused_computation.55 | convolution fusion | flops 6450839552 | bytes 16789504 | tf_op jit(solution)/shard_map/dot_general | solution.py:64
  30.3 1.7 slice.51
  31.9 1.6 copy-done.9
  33.7 0.6 gather_fusion.3
  34.4 0.6 gather_fusion.4
  35.1 0.6 gather_fusion
  36.2 1.8 gather_fusion.2
  37.9 36.9 %all-gather.6.cloned.1.call-done = bf16[64,16,2048]{2,1,0:T(8,128)(2,1)} async-done(((bf16[8,16,2048]{2,1,0:T(8,128)(2,1)}), bf16[64,16,2048]{2,1,0:T(8,128)(2,1)}) %all-gather.6.cloned.1.call-update) | async-done | bytes 4194320 | tf_op jit(solution)/shard_map/all_gather | solution.py:70
  74.8 2.7 gather_fusion.1
  77.6 5.8 fusion.61
  83.3 2.9 subtract_convert_fusion
  86.2 1.5 pad_maximum_fusion
  87.8 28.0 %while.11 = (s32[]{:T(128)}, bf16[2,512,8,64]{1,3,2,0:T(8,128)(2,1)}, bf16[2,512,8,64]{1,3,2,0:T(8,128)(2,1)S(1)}, s32[2]{0:T(128)S(1)}, bf16[2,512,8,64]{1,3,2,...) while((s32[]{:T(128)}, bf16[2,512,8,64]{1,3,2,0:T(8,128)(2,1)}, ...), condition=%wide.region_4.6_spmd.clone, body=%wide.region_1.5_spmd.clone.sunk | while | flops 550241280 | bytes 19434588 | solution.py:106
  87.8 0.6 dynamic_slice.68
  88.3 0.6 iota_compare_fusion.5
  89.1 7.6 %fusion.116 = (f32[8,512]{1,0:T(8,128)S(1)}, f32[8,512,512]{1,2,0:T(8,128)}) fusion(pred[512,512]{0,1:T(8,128)(4,1)S(1)} %fusion.115, bf16[2,512,8,64]{1,3,2,0:T(8,128)(2,1)} %get-tuple-element.155, s32[]{:T(128)} %get-tuple-element.143, bf16[2,512,8,64]{1,3,2,0:T(8,128)(2,1)} %get-tuple-element.154), kind=kOutput, calls=%fused_computation.116.clone.1 | convolution fusion | flops 276824576 | bytes 9716736 | tf_op jit(solution)/shard_map/while/body/eval_jaxpr/sub | solution.py:101
  96.7 5.0 fusion.117
  101.8 0.6 dynamic_slice.68
  102.3 0.6 iota_compare_fusion.5
  103.1 7.6 %fusion.116 = (f32[8,512]{1,0:T(8,128)S(1)}, f32[8,512,512]{1,2,0:T(8,128)}) fusion(pred[512,512]{0,1:T(8,128)(4,1)S(1)} %fusion.115, bf16[2,512,8,64]{1,3,2,0:T(8,128)(2,1)} %get-tuple-element.155, s32[]{:T(128)} %get-tuple-element.143, bf16[2,512,8,64]{1,3,2,0:T(8,128)(2,1)} %get-tuple-element.154), kind=kOutput, calls=%fused_computation.116.clone.1 | convolution fusion | flops 276824576 | bytes 9716736 | tf_op jit(solution)/shard_map/while/body/eval_jaxpr/sub | solution.py:101
  110.7 5.0 fusion.117
  115.7 2.3 copy.27
  118.3 4.4 convolution_convert_fusion
  123.3 0.5 all-gather.12.cloned.1.call-update
  123.9 153.9 %all-reduce.4.cloned.1.call-done = bf16[2,512,2048]{2,1,0:T(8,128)(2,1)} async-done(((bf16[2,512,2048]{2,1,0:T(8,128)(2,1)}), bf16[2,512,2048]{2,1,0:T(8,128)(2,1)}) %all-reduce.4.cloned.1.call-update) | async-done | bytes 4194320 | tf_op jit(solution)/shard_map/psum | solution.py:110
  277.9 5.0 fusion.48
  282.9 0.9 copy-done.6
  283.8 3.6 fusion.50
  287.4 45.8 %all-gather.10.cloned.1.call-done = bf16[2048,2,1024]{2,1,0:T(2,128)(2,1)} async-done(((bf16[256,2,1024]{2,1,0:T(2,128)(2,1)}), bf16[2048,2,1024]{2,1,0:T(2,128)(2,1)}) %all-gather.10.cloned.1.call-update) | async-done | bytes 8388624 | tf_op jit(solution)/shard_map/all_gather | solution.py:119
  333.2 10.4 %copy.33 = bf16[256,8,2,1024]{3,1,2,0:T(8,128)(2,1)} copy(bf16[256,8,2,1024]{3,2,1,0:T(2,128)(2,1)} %bitcast.100) | data formatting | bytes 16777216
  343.5 13.2 %fusion.97 = f32[1024,2048]{1,0:T(8,128)} fusion(bf16[1024,2048]{1,0:T(8,128)(2,1)S(1)} %bitcast.102, bf16[2048,2048]{1,0:T(8,128)(2,1)} %bitcast.101), kind=kOutput, calls=%fused_computation.117 | convolution fusion | flops 8589934592 | bytes 20971520 | tf_op jit(solution)/shard_map/dot_general | solution.py:120
  356.8 15.8 %all-gather.12.cloned.1.call-done = bf16[1024,2048]{1,0:T(8,128)(2,1)} async-done(((bf16[1024,256]{1,0:T(8,128)(2,1)}), bf16[1024,2048]{1,0:T(8,128)(2,1)}) %all-gather.12.cloned.1.call-update) | async-done | bytes 4194320 | tf_op jit(solution)/shard_map/all_gather | solution.py:128
  372.5 11.2 %convolution_convert_fusion.1 = bf16[1024,2048]{1,0:T(8,128)(2,1)} fusion(bf16[1024,2048]{1,0:T(8,128)(2,1)} %all-gather.12.cloned.1.call-done, f32[1024,2048]{1,0:T(8,128)} %fusion.97), kind=kOutput, calls=%fused_computation.61 | convolution fusion | flops 4303355904 | bytes 16777216 | tf_op jit(solution)/shard_map/dot_general | solution.py:126
  383.8 0.6 copy-done.14
  384.4 0.6 dynamic-slice
  385.8 153.1 %all-reduce.6.cloned.1.call-done = bf16[2,512,2048]{2,1,0:T(8,128)(2,1)} async-done(((bf16[2,512,2048]{2,1,0:T(8,128)(2,1)}), bf16[2,512,2048]{2,1,0:T(8,128)(2,1)}) %all-reduce.6.cloned.1.call-update) | async-done | bytes 4194320 | tf_op jit(solution)/shard_map/psum | solution.py:131
  538.9 6.9 %multiply_reduce_fusion = (f32[2]{0:T(128)S(1)}, bf16[2,512,2048]{2,1,0:T(8,128)(2,1)S(1)}) fusion(bf16[2,512,2048]{2,1,0:T(8,128)(2,1)} %all-reduce.6.cloned.1.call-done, bf16[2,512,2048]{2,1,0:T(8,128)(2,1)} %all-reduce.4.cloned.1.call-done, bf16[2,512,2048]{2,1,0:T(8,128)(2,1)} %param.19, pred[2,512]{1,0:T(4,128)(4,1)S(1)} %iota_compare_fusion.3), kind=kLoop, calls=%fused_computation.54 | loop fusion | flops 25165822 | bytes 16778248 | tf_op jit(solution)/shard_map/reduce_sum | solution.py:136
  545.9 2.0 copy-done.7
  547.9 0.7 fusion.82
  548.8 9.2 %all-gather = bf16[8,2,2048]{2,1,0:T(2,128)(2,1)S(1)} all-gather(bf16[1,2,2048]{2,1,0:T(2,128)(2,1)S(1)} %bitcast.109), channel_id=1, replica_groups=mesh['req'=8,'mlp'=4] {'req'}, dimensions={0}, use_global_device_ids=true | all-gather | bytes 73728 | tf_op jit(solution)/shard_map/all_gather | solution.py:143
  558.0 4.6 convolution_reduce_fusion
  562.8 38.2 %pmax.7 = f32[16]{0:T(128)S(1)} all-reduce(f32[16]{0:T(128)S(1)} %convolution_reduce_fusion), channel_id=1, replica_groups=mesh['req'=8,'mlp'=4] {'req','mlp'}, use_global_device_ids=true, to_apply=%region_12.14 | all-reduce | flops 16 | bytes 128 | tf_op jit(solution)/shard_map/pmax | solution.py:152
  601.0 12.7 %all-reduce = f32[16]{0:T(128)S(1)} all-reduce(f32[16]{0:T(128)S(1)} %sqrt_dynamic-update-slice_fusion), channel_id=1, replica_groups=mesh['req'=8,'mlp'=4] {'req'}, use_global_device_ids=true, to_apply=%add | all-reduce | flops 16 | bytes 128
  613.7 0.6 select_reduce_fusion
  (59 shorter events, 2.9 us)
Async XLA Ops:
  7.2 111.1 %copy-start = (bf16[512,2048]{1,0:T(8,128)(2,1)S(1)}, bf16[512,2048]{1,0:T(8,128)(2,1)}, u32[]{:S(2)}) copy-start(bf16[512,2048]{1,0:T(8,128)(2,1)} %param.28) | copy-start | bytes 6291460
  7.2 29.0 %all-gather.8.cloned.1.call-start = ((), (), s32[]{:S(2)}) async-start(), calls=%async_computation.1 | async-start | bytes 1179648 | tf_op jit(solution)/shard_map/all_gather | solution.py:71
  7.9 66.9 %all-gather.6.cloned.1.call-start = ((), (), s32[]{:S(2)}) async-start(), calls=%async_computation | async-start | bytes 4718592 | tf_op jit(solution)/shard_map/all_gather | solution.py:70
  8.7 269.2 %all-reduce.4.cloned.1.call-start = ((), (), s32[]{:S(2)}) async-start(), calls=%async_computation.2 | async-start | bytes 8388608 | tf_op jit(solution)/shard_map/psum | solution.py:110
  17.5 3.6 copy-start.4
  17.5 3.6 copy-start.13
  30.2 3.3 copy-start.9
  30.2 3.4 copy-start.12
  30.2 3.5 copy-start.1
  30.2 4.1 copy-start.2
  30.2 4.9 copy-start.3
  122.7 210.5 %all-gather.10.cloned.1.call-start = ((), (), s32[]{:S(2)}) async-start(), calls=%async_computation.3 | async-start | bytes 9437184 | tf_op jit(solution)/shard_map/all_gather | solution.py:119
  123.3 249.2 %all-gather.12.cloned.1.call-start = ((), (), s32[]{:S(2)}) async-start(), calls=%async_computation.4 | async-start | bytes 4718592 | tf_op jit(solution)/shard_map/all_gather | solution.py:128
  123.9 159.0 %copy-start.10 = (f32[2048]{0:T(1024)S(1)}, f32[2048]{0:T(1024)}, u32[]{:S(2)}) copy-start(f32[2048]{0:T(1024)} %param.25) | copy-start | bytes 24580
  123.9 415.0 %all-reduce.6.cloned.1.call-start = ((), (), s32[]{:S(2)}) async-start(), calls=%async_computation.5 | async-start | bytes 8388608 | tf_op jit(solution)/shard_map/psum | solution.py:131
  277.8 5.1 copy-start.5
  277.9 5.9 copy-start.6
  333.2 10.4 %copy-start.8 = (bf16[2,512,2048]{2,1,0:T(8,128)(2,1)S(1)}, bf16[2,512,2048]{2,1,0:T(8,128)(2,1)}, u32[]{:S(2)}) copy-start(bf16[2,512,2048]{2,1,0:T(8,128)(2,1)} %fusion.50) | copy-start | bytes 12582916
  383.7 0.7 copy-start.14
  545.9 2.0 copy-start.7
  545.9 2.8 copy-start.11
Sparse Core Ops, SparseCore 0:
  9.9 26.2 all-gather.7
  38.0 36.7 all-gather.5
  122.8 154.9 all-reduce.3
  279.8 53.3 all-gather.9
  335.1 37.4 all-gather.11
  383.9 154.9 all-reduce.5
where the time goes:
time: 622 us; the launch traced here: 621 us
  waiting for transfers between devices  408 us (66%)
  matrix products  74.2 us (12%)
  blocking collectives  60.2 us (10%)
  local copies, waits for them, and re-layouts  37.1 us (6%)
  other arithmetic  26.5 us (4%)
  between operations  15 us (2%)
    psum x1, waiting for transfers between devices, per_device(): lax.psum(head_part.astype(jnp.bfloat16), 'mlp').astype(jnp.float32)  154 us
    psum x1, waiting for transfers between devices, per_device(): lax.psum(unit_part.astype(jnp.bfloat16), 'mlp').astype(jnp.float32)  153 us
    all_gather x1, waiting for transfers between devices, per_device(): shard_piece = lax.all_gather(w_gateup, 'req', axis=0, tiled=True)  45.8 us
    pmax x1, blocking collectives, per_device(): slot_peak = lax.pmax(jnp.max(logits, axis=1), ('req', 'mlp'))  38.2 us
    all_gather x1, waiting for transfers between devices, per_device(): lax.all_gather(adapter_down, 'req', axis=0, tiled=True)  36.9 us
    unnamed x35, local copies, waits for them, and re-layouts  25.4 us
    all_gather x1, waiting for transfers between devices, per_device(): lax.all_gather(w_down, 'req', axis=1, tiled=True)  15.8 us
    sub x2, matrix products, attend(): probabilities = jax.nn.softmax(scores, axis=-1).astype(jnp.bfloat16)  15.1 us
  transfers between devices with their start and end apart: 6, of which 6 were waited for; matrix products, arithmetic and copies ran while one was open for 10% of the time, Pallas kernels for 0%

commit v1 on v0

v1 whole, which is shorter than its diff:
```python
import functools
import math

import jax
import jax.numpy as jnp
import numpy as np
from jax import lax
from jax.experimental import pallas as pl
from jax.experimental.pallas import tpu as pltpu
from jax.sharding import PartitionSpec as P

HEAD_WIDTH = 64
EPSILON = 1e-05
ROPE_BASE = 130000.0
ADAPTER_SCALE = 2.0
MASKED = -1e30
F32, BF16 = jnp.float32, jnp.bfloat16
VMEM_LIMIT = 56 * 1024 * 1024

ME, Z, CORE, LENS = 0, 1, 2, 4
LAST_ROWS = 16


def nt(a, b):
    return lax.dot_general(a, b, (((1,), (1,)), ((), ())), preferred_element_type=F32)


def nn(a, b):
    return jnp.dot(a, b, preferred_element_type=F32)


def call(kernel, grid, ins, outs, shapes, scratch=(), flops=0, nbytes=0):
    spec = pltpu.PrefetchScalarGridSpec(
        num_scalar_prefetch=1, grid=grid, in_specs=ins, out_specs=outs, scratch_shapes=scratch
    )
    return pl.pallas_call(
        kernel,
        grid_spec=spec,
        out_shape=shapes,
        compiler_params=pltpu.CompilerParams(vmem_limit_bytes=VMEM_LIMIT),
        cost_estimate=pl.CostEstimate(
            flops=int(flops), bytes_accessed=int(nbytes), transcendentals=0
        ),
    )


def whole(shape):
    zeros = (0,) * len(shape)
    return pl.BlockSpec(tuple(shape), lambda *_: zeros)


def rope_tables(length):
    half = HEAD_WIDTH // 2
    frequency = np.float32(ROPE_BASE) ** (-(np.arange(half, dtype=np.float32) * 2.0 / HEAD_WIDTH))
    angles = np.arange(length, dtype=np.float32)[:, None] * frequency.astype(np.float32)[None, :]
    angles = angles.astype(np.float32)
    cosine, sine = np.cos(angles), np.sin(angles)
    return (
        np.concatenate([cosine] * 4, axis=1).astype(np.float32),
        np.concatenate([-sine, sine, -sine, sine], axis=1).astype(np.float32),
    )


def rotate(block, cosine, sine):
    lane = lax.broadcasted_iota(jnp.int32, block.shape, 1)
    front = (lane % HEAD_WIDTH) < HEAD_WIDTH // 2
    partner = jnp.where(
        front, pltpu.roll(block, 128 - HEAD_WIDTH // 2, 1), pltpu.roll(block, HEAD_WIDTH // 2, 1)
    )
    return block * cosine + partner * sine


def pick_kernel(slots, rows_at, table_rows, width, info, down, up, *outs):
    for j, out in enumerate(outs):
        for s in range(slots):
            slot = (info[ME] ^ j) * slots + s
            row = lax.rem(info[rows_at + slot], table_rows)
            out[s, :, :width] = down[row]
            out[s, :, width:] = up[row]


def project_kernel(
    info, x_ref, gain_ref, w_ref, cos_ref, sin_ref, k_ref, v_ref, q_ref, normed_ref, held
):
    part, i = pl.program_id(0), pl.program_id(1)
    rows = x_ref.shape[0]
    at = pl.ds(pl.multiple_of(i * rows, rows), rows)

    @pl.when(part == 0)
    def _():
        x = x_ref[...].astype(F32)
        mean = jnp.mean(x * x, axis=-1, keepdims=True)
        normed = (x * lax.rsqrt(mean + EPSILON) * gain_ref[...]).astype(BF16)
        held[at] = normed
        normed_ref[...] = normed

    product = nn(held[at], w_ref[0])

    @pl.when(part == 0)
    def _():
        for g in range(product.shape[1] // 128):
            lanes = slice(g * 128, g * 128 + 128)
            k_ref[:, lanes] = rotate(product[:, lanes], cos_ref[...], sin_ref[...]).astype(BF16)

    @pl.when(part == 1)
    def _():
        v_ref[...] = product.astype(BF16)

    @pl.when(part == 2)
    def _():
        q_ref[...] = product


def attend_kernel(
    slots, rows_at, table_rows, n, info, q_ref, k_ref, v_ref, normed_ref, cos_ref, sin_ref, *rest
):
    received, (out_ref, queries, factors) = rest[:n], rest[n:]
    s = pl.program_id(0)
    length, columns = q_ref.shape
    width = normed_ref.shape[1]
    table_row = info[rows_at + info[ME] * slots + s]
    source = info[ME] ^ lax.div(table_row, table_rows)
    for j in range(n):

        @pl.when(source == j)
        def _(j=j):
            factors[...] = received[j][s]

    low_rank = nt(normed_ref[...], factors[:, :width]).astype(BF16)
    raised = nn(low_rank, factors[:, width:])
    full = q_ref[...] + ADAPTER_SCALE * raised
    for g in range(columns // 128):
        lanes = slice(g * 128, g * 128 + 128)
        queries[:, lanes] = rotate(full[:, lanes], cos_ref[...], sin_ref[...]).astype(BF16)
    step = 128
    scale = HEAD_WIDTH ** (-0.5) * math.log2(math.e)

    def pair(g, carry):
        lanes = pl.ds(pl.multiple_of(g * 128, 128), 128)
        for b in range(length // step):
            keys = (b + 1) * step
            q = queries[b * step : keys, lanes]
            first = lax.broadcasted_iota(jnp.int32, q.shape, 1) < HEAD_WIDTH
            zero = jnp.zeros_like(q)
            both = jnp.concatenate([jnp.where(first, q, zero), jnp.where(first, zero, q)], axis=0)
            scores = nt(both, k_ref[0:keys, lanes]) * scale
            row = lax.broadcasted_iota(jnp.int32, scores.shape, 0) % step + b * step
            col = lax.broadcasted_iota(jnp.int32, scores.shape, 1)
            scores = jnp.where(col <= row, scores, MASKED)
            top = jnp.max(scores, axis=1, keepdims=True)
            weights = jnp.exp2(scores - top)
            total = jnp.sum(weights, axis=1, keepdims=True)
            mixed = nn(weights.astype(BF16), v_ref[0:keys, lanes]) / total
            out_ref[b * step : keys, lanes] = jnp.where(first, mixed[:step], mixed[step:]).astype(
                BF16
            )
        return carry

    lax.fori_loop(0, columns // 128, pair, 0)


def targets(info, row, slots, length, core):
    place = jnp.full(row.shape, -1, jnp.int32)
    for s in range(slots):
        g = core * slots + s
        live = info[LENS + g]
        off = info[LENS + 2 * slots + g]
        inside = (row >= off) & (row < off + live)
        place = jnp.where(inside, row - off + s * length, place)
        place = jnp.where(row == g, s * length + live - 1, place)
    return place


def one_hot(place, columns):
    col = lax.broadcasted_iota(jnp.int32, (place.shape[0], columns), 1)
    return jnp.where(col == place, 1.0, 0.0).astype(BF16)


def hidden_kernel(slots, nz, starts, sizes, info, hidden_ref, *outs):
    count = len(sizes)
    length = hidden_ref.shape[0] // slots
    core = info[CORE]
    for k in range(count):
        quarter = sizes[k] // nz
        for whose in range(2):
            target_core = core if whose == 0 else 1 - core
            base = starts[k] * 2 + target_core * sizes[k] + info[Z] * quarter
            row = lax.broadcasted_iota(jnp.int32, (quarter, 1), 0) + base
            place = targets(info, row, slots, length, core)
            outs[whose * count + k][...] = nn(
                one_hot(place, hidden_ref.shape[0]), hidden_ref[...]
            ).astype(BF16)


def mix_kernel(slots, start, size, info, own_ref, other_ref, w_ref, out_ref):
    length = own_ref.shape[0] // slots
    core = info[CORE]
    row = lax.broadcasted_iota(jnp.int32, (size, 1), 0) + start * 2 + core * size
    packed = nn(
        one_hot(targets(info, row, slots, length, core), own_ref.shape[0]), own_ref[...]
    ) + nn(
        one_hot(targets(info, row, slots, length, 1 - core), own_ref.shape[0]), other_ref[...]
    )
    product = nn(packed.astype(BF16), w_ref[...]).astype(BF16)
    out_ref[...] = product.reshape(out_ref.shape)


def stream_kernel(info, part_ref, right, left, own, other, gain, stream_ref, normed_ref):
    mixed = part_ref[0].astype(F32) + right[...].astype(F32) + left[...].astype(F32)
    hidden = own[...].astype(F32) + other[...].astype(F32)
    stream = (hidden + mixed).astype(BF16)
    stream_ref[...] = stream
    x = stream.astype(F32)
    mean = jnp.mean(x * x, axis=-1, keepdims=True)
    normed_ref[...] = (x * lax.rsqrt(mean + EPSILON) * gain[...]).astype(BF16)


def finish_kernel(slots, start, size, info, part_ref, right, left, stream, out_ref, sums_ref):
    quarter, width = stream.shape
    total = part_ref[0].astype(F32) + right[...].astype(F32) + left[...].astype(F32)
    result = stream[...].astype(F32) + total
    row = lax.broadcasted_iota(jnp.int32, (quarter, 1), 0)
    row = row + start * 2 + info[CORE] * size + info[Z] * quarter
    keep = row < 2 * slots
    belongs = []
    for g in range(2 * slots):
        live, off = info[LENS + g], info[LENS + 2 * slots + g]
        inside = (row >= off) & (row < off + live)
        belongs.append(inside)
        keep = keep | inside
    rounded = jnp.where(keep, result, 0.0).astype(BF16)
    out_ref[...] = rounded
    wide = rounded.astype(F32)
    squares = jnp.sum(wide * wide, axis=1, keepdims=True)
    lane = lax.broadcasted_iota(jnp.int32, sums_ref.shape, 1)
    sums = jnp.zeros(sums_ref.shape, F32)
    for g in range(2 * slots):
        sums = jnp.where(lane == g, jnp.sum(jnp.where(belongs[g], squares, 0.0)), sums)
    sums_ref[...] = sums


def unit_kernel(nz, info, own, *rest):
    rights, lefts = rest[: nz - 1], rest[nz - 1 : 2 * nz - 2]
    w_ref, out_ref, x, acc = rest[2 * nz - 2 :]
    b = pl.program_id(0)
    quarter = own.shape[0]
    z = info[Z]

    @pl.when(b == 0)
    def _():
        for place in range(nz):
            at = slice(place * quarter, (place + 1) * quarter)

            @pl.when(z == place)
            def _(at=at):
                x[at] = own[...]

            for d in range(1, nz):

                @pl.when(z - place == d)
                def _(at=at, d=d):
                    x[at] = rights[d - 1][...]

                @pl.when(place - z == d)
                def _(at=at, d=d):
                    x[at] = lefts[d - 1][...]

    depth = w_ref.shape[1] // 3
    columns = w_ref.shape[2]
    width = x.shape[1]
    gate = nn(x[...], w_ref[:, 0:depth].reshape(width, columns))
    up = nn(x[...], w_ref[:, depth : 2 * depth].reshape(width, columns))
    active = (gate / (1.0 + jnp.exp(-gate)) * up).astype(BF16)
    product = nt(active, w_ref[:, 2 * depth :].reshape(width, columns))

    @pl.when(b == 0)
    def _():
        acc[...] = product

    @pl.when(b > 0)
    def _():
        acc[...] += product

    @pl.when(b == pl.num_programs(0) - 1)
    def _():
        out_ref[...] = acc[...].astype(BF16).reshape(out_ref.shape)


def take(parts, index):
    return lax.dynamic_index_in_dim(parts, index, 0, keepdims=False)


def reduce_to_owners(parts, z, nz):
    right = left = None
    for s in range(1, nz):
        message = take(parts, jnp.clip(nz - s + z, 0, nz - 1))
        right = lax.ppermute(
            message if right is None else message + right, "mlp", [(i, i + 1) for i in range(s)]
        )
        message = take(parts, jnp.clip(s + z - nz, 0, nz - 1))
        left = lax.ppermute(
            message if left is None else message + left,
            "mlp",
            [(nz - 1 - i, nz - 2 - i) for i in range(s)],
        )
    return right, left


def spread(own, nz):
    rights, lefts = [own], [own]
    for s in range(1, nz):
        rights.append(lax.ppermute(rights[-1], "mlp", [(i, i + 1) for i in range(s - 1, nz - 1)]))
        lefts.append(lax.ppermute(lefts[-1], "mlp", [(i + 1, i) for i in range(0, nz - s)]))
    return rights[1:], lefts[1:]


def body(total, info, hidden, slot_request, gains, w_qkv, w_out, merged, tables, vocab, sizes_n):
    n, nz = sizes_n
    gain_attn, gain_mlp, final_gain = gains
    down, up = tables
    slots, length, width = hidden.shape
    rows = slots * length
    columns = w_qkv.shape[2]
    rank = down.shape[1]
    table_rows = down.shape[0]
    rows_at = LENS + 4 * slots
    me, z = lax.axis_index("req"), lax.axis_index("mlp")
    core = me % 2
    swap = [(i, i ^ 1) for i in range(n)]
    half = -(-total // 128) * 64
    sizes = [half, total - half]
    starts = [0, half]
    count = len(sizes)

    weights = lax.all_gather(merged, "req", axis=0)

    factor_shape = (slots, rank, width + columns)
    picked = call(
        functools.partial(pick_kernel, slots, rows_at, table_rows, width),
        (1,),
        [whole(down.shape), whole(up.shape)],
        [whole(factor_shape)] * n,
        [jax.ShapeDtypeStruct(factor_shape, BF16)] * n,
    )(info, down, up)
    received = [picked[0]] + [
        lax.ppermute(picked[j], "req", [(i, i ^ j) for i in range(n)]) for j in range(1, n)
    ]

    cosine, sine = rope_tables(length)
    block = 256
    blocks = rows // block
    per_slot = length // block
    last = blocks - 1
    keys, values, queries, normed = call(
        project_kernel,
        (3, blocks),
        [
            pl.BlockSpec((block, width), lambda p, i, _: (jnp.where(p == 0, i, last), 0)),
            whole((1, width)),
            pl.BlockSpec((1, width, columns), lambda p, i, _: ((p + 1) % 3, 0, 0)),
            pl.BlockSpec((block, 128), lambda p, i, _: (i % per_slot, 0)),
            pl.BlockSpec((block, 128), lambda p, i, _: (i % per_slot, 0)),
        ],
        [
            pl.BlockSpec((block, columns), lambda p, i, _: (jnp.where(p == 0, i, last), 0)),
            pl.BlockSpec(
                (block, columns),
                lambda p, i, _: (jnp.where(p == 0, 0, jnp.where(p == 1, i, last)), 0),
            ),
            pl.BlockSpec((block, columns), lambda p, i, _: (jnp.where(p == 2, i, 0), 0)),
            pl.BlockSpec((block, width), lambda p, i, _: (jnp.where(p == 0, i, last), 0)),
        ],
        [
            jax.ShapeDtypeStruct((rows, columns), BF16),
            jax.ShapeDtypeStruct((rows, columns), BF16),
            jax.ShapeDtypeStruct((rows, columns), F32),
            jax.ShapeDtypeStruct((rows, width), BF16),
        ],
        [pltpu.VMEM((rows, width), BF16)],
        flops=2 * rows * width * 3 * columns,
        nbytes=2 * (2 * rows * width + 3 * width * columns),
    )(info, hidden.reshape(rows, width), gain_attn, w_qkv, cosine, sine)

    by_slot = lambda w: pl.BlockSpec((length, w), lambda s, _: (s, 0))
    attended = call(
        functools.partial(attend_kernel, slots, rows_at, table_rows, n),
        (slots,),
        [by_slot(columns)] * 3
        + [by_slot(width), whole((length, 128)), whole((length, 128))]
        + [whole(factor_shape)] * n,
        by_slot(columns),
        jax.ShapeDtypeStruct((rows, columns), BF16),
        [pltpu.VMEM((length, columns), BF16), pltpu.VMEM(factor_shape[1:], BF16)],
        flops=8 * rows * length * columns,
        nbytes=2 * rows * (width + 5 * columns),
    )(info, queries, keys, values, normed, cosine, sine, *received)
    other = lax.ppermute(attended, "req", swap)

    quarters = [size // nz for size in sizes]
    quarter_shapes = [jax.ShapeDtypeStruct((q, width), BF16) for q in quarters]
    quarter_specs = [whole((q, width)) for q in quarters]
    shared = call(
        functools.partial(hidden_kernel, slots, nz, starts, sizes),
        (1,),
        [whole((rows, width))],
        quarter_specs * 2,
        quarter_shapes * 2,
        flops=4 * sum(quarters) * rows * width,
        nbytes=2 * rows * width,
    )(info, hidden.reshape(rows, width))
    hidden_own = shared[:count]
    hidden_other = [lax.ppermute(piece, "req", swap) for piece in shared[count:]]

    def own_part(q):
        return pl.BlockSpec((1, q, width), lambda i, info: (info[Z], 0, 0))

    outs, sums = [], 0.0
    for k in range(count):
        q, size, spec = quarters[k], sizes[k], quarter_specs[k]
        part_shape = jax.ShapeDtypeStruct((nz, q, width), BF16)
        head_parts = call(
            functools.partial(mix_kernel, slots, starts[k], size),
            (1,),
            [whole((rows, columns))] * 2 + [whole(w_out.shape)],
            whole(part_shape.shape),
            part_shape,
            flops=2 * size * columns * (2 * rows + width),
            nbytes=2 * (columns * (2 * rows + width) + size * width),
        )(info, attended, other, w_out)
        right, left = reduce_to_owners(head_parts, z, nz)
        stream, mid = call(
            stream_kernel,
            (1,),
            [own_part(q)] + [spec] * 4 + [whole((1, width))],
            [spec, spec],
            [quarter_shapes[k]] * 2,
            nbytes=14 * q * width,
        )(info, head_parts, right, left, hidden_own[k], hidden_other[k], gain_mlp)
        rights, lefts = spread(mid, nz)
        unit = 256
        unit_parts = call(
            functools.partial(unit_kernel, nz),
            (weights.shape[2] // unit,),
            [spec] * (2 * nz - 1)
            + [pl.BlockSpec(weights.shape[:2] + (unit,), lambda b, _: (0, 0, b))],
            whole(part_shape.shape),
            part_shape,
            [pltpu.VMEM((size, width), BF16), pltpu.VMEM((size, width), F32)],
            flops=6 * size * width * weights.shape[2],
            nbytes=2 * weights.size,
        )(info, mid, *rights, *lefts, weights)
        right, left = reduce_to_owners(unit_parts, z, nz)
        out, sum_k = call(
            functools.partial(finish_kernel, slots, starts[k], size),
            (1,),
            [own_part(q)] + [spec] * 3,
            [spec, whole((8, 128))],
            [quarter_shapes[k], jax.ShapeDtypeStruct((8, 128), F32)],
            nbytes=10 * q * width,
        )(info, unit_parts, right, left, stream)
        sums = sums + sum_k
        rights, lefts = spread(out, nz)
        line = jnp.concatenate(rights[::-1] + [out] + lefts, axis=0)
        mine = lax.dynamic_slice_in_dim(line, (nz - 1 - z) * q, nz * q, 0)
        theirs = lax.ppermute(mine, "req", swap)
        outs.append(jnp.where(core == 0, mine, theirs))
        outs.append(jnp.where(core == 0, theirs, mine))

    slots_all = slot_request.shape[0]
    chip_rows = outs[0][: 2 * slots].astype(F32)
    chip_last = (
        chip_rows
        * lax.rsqrt(jnp.mean(chip_rows * chip_rows, axis=-1, keepdims=True) + EPSILON)
        * final_gain
    ).astype(BF16)
    every = jnp.zeros((slots_all, width), BF16)
    every = lax.dynamic_update_slice_in_dim(every, chip_last, (me // 2) * 2 * slots, 0)
    bit = 2
    while bit < n:
        every = every + lax.ppermute(every, "req", [(i, i ^ bit) for i in range(n)])
        bit *= 2
    peaks = jnp.max(nt(every, vocab), axis=1)
    norm_sums = jnp.zeros((slots_all,), F32)
    norm_sums = lax.dynamic_update_slice_in_dim(
        norm_sums, sums[0, : 2 * slots], (me // 2) * 2 * slots, 0
    )
    bit = 1
    while bit < n * nz:
        if bit < n:
            axis, pairs = "req", [(i, i ^ bit) for i in range(n)]
        else:
            axis, pairs = "mlp", [(i, i ^ (bit // n)) for i in range(nz)]
        arrived = lax.ppermute(jnp.stack([norm_sums, peaks]), axis, pairs)
        norm_sums = norm_sums + arrived[0]
        peaks = jnp.maximum(peaks, arrived[1])
        bit *= 2

    packed = jnp.concatenate(outs + [jnp.zeros((length, width), BF16)], axis=0)
    result = []
    for s in range(slots):
        g = core * slots + s
        piece = lax.dynamic_slice_in_dim(packed, info[LENS + 2 * slots + g], length, 0)
        live = jnp.arange(length, dtype=jnp.int32) < info[LENS + g]
        result.append(jnp.where(live[:, None], piece, jnp.zeros((), BF16)))
    return jnp.stack(result), norm_sums, peaks


def per_device(sizes_n, *arrays):
    (hidden, lengths, slot_request, adapter_of, adapter_slot, gain_attn, gain_mlp, final_gain) = (
        arrays[:8]
    )
    (w_qkv, w_out, w_gateup, w_down, adapter_down, adapter_up, vocab) = arrays[8:]
    slots, length, width = hidden.shape
    me, z = lax.axis_index("req"), lax.axis_index("mlp")

    def look_up(table, index):
        at = jnp.arange(table.shape[0], dtype=jnp.int32)
        return jnp.sum(jnp.where(index[:, None] == at[None, :], table[None, :], 0), axis=1)

    slot_lengths = look_up(lengths, slot_request)
    table_rows = look_up(adapter_slot, look_up(adapter_of, slot_request))
    aligned = ((slot_lengths + 15) // 16 * 16).reshape(-1, 2 * slots)
    before = jnp.arange(2 * slots)[:, None] < jnp.arange(2 * slots)[None, :]
    offsets = LAST_ROWS + jnp.sum(
        jnp.where(before[None], aligned[:, :, None], 0), axis=1, dtype=jnp.int32
    )
    needed = jnp.max(LAST_ROWS + jnp.sum(aligned, axis=1))
    chip = jnp.arange(aligned.shape[0]) == me // 2
    own = lambda values: jnp.sum(
        jnp.where(chip[:, None], values.reshape(-1, 2 * slots), 0), axis=0, dtype=jnp.int32
    )
    info = jnp.concatenate(
        [
            jnp.stack([me, z, me % 2, needed]).astype(jnp.int32),
            own(slot_lengths),
            own(offsets),
            table_rows,
        ]
    )
    merged = jnp.concatenate([w_gateup[:, 0], w_gateup[:, 1], w_down.T], axis=0)
    largest = -(-(2 * slots * length + LAST_ROWS) // 128) * 64
    out, norm_sums, peaks = body(
        largest,
        info,
        hidden,
        slot_request,
        tuple(g.reshape(1, width) for g in (gain_attn, gain_mlp, final_gain)),
        w_qkv.transpose(1, 0, 2),
        w_out,
        merged,
        (adapter_down, adapter_up),
        vocab,
        sizes_n,
    )
    slot_norm = jnp.sqrt(norm_sums / (slot_lengths.astype(F32) * width))
    requests = jnp.arange(slot_request.shape[0], dtype=jnp.int32)
    owners = slot_request[None, :] == requests[:, None]
    request_norm = jnp.sum(jnp.where(owners, slot_norm[None, :], 0.0), axis=1)
    request_peak = jnp.sum(jnp.where(owners, peaks[None, :], 0.0), axis=1)
    return out, request_norm, request_peak


def solution(mesh):
    return jax.shard_map(
        functools.partial(per_device, (mesh.shape["req"], mesh.shape["mlp"])),
        mesh=mesh,
        in_specs=(
            P("req", None, None),
            P(),
            P(),
            P(),
            P(),
            P(),
            P(),
            P(),
            P(None, None, "mlp"),
            P("mlp", None),
            P("req", None, "mlp"),
            P("mlp", "req"),
            P("req", None, None),
            P("req", None, "mlp"),
            P(("req", "mlp"), None),
        ),
        out_specs=(P("req", None, None), P(), P()),
        check_vma=False,
    )
```

time: 622 us -> 536 us (0.86); the launches traced: 621 us -> 526 us
  waiting for transfers between devices: 408 us -> 167 us
  starting transfers between devices: 0.23 us -> 148 us
  Pallas kernels: 0 us -> 103 us
  matrix products: 74.2 us -> 4.77 us
  blocking collectives: 60.2 us -> 0 us
  local copies, waits for them, and re-layouts: 37.1 us -> 53.8 us
    psum x2 -> x0, waiting for transfers between devices: 307 us -> none  [the longest x1 154 us: per_device(): lax.psum(head_part.astype(jnp.bfloat16), 'mlp').astype(jnp.float32)]
    ppermute x0 -> x67, waiting for transfers between devices: none -> 167 us  [the longest x12 74.1 us: spread(): lax.ppermute(lefts[-1], 'mlp', [(i + 1, i) for i in range(0, nz - s)])]
    ppermute x0 -> x67, starting transfers between devices: none -> 148 us  [the longest x12 77.5 us: reduce_to_owners(): lax.ppermute(message if right is None else message + right, 'mlp', [(i, i...]
    pallas_call x0 -> x12, Pallas kernels: none -> 103 us  [the longest x2 29.6 us: body(): call(functools.partial(unit_kernel, nz), (weights.shape[2] // unit,), [sp...]
    all_gather x4 -> x1, waiting for transfers between devices: 98.5 us -> 0.02 us  [body(): weights = lax.all_gather(merged, 'req', axis=0)]
    dot_general x9 -> x1, matrix products: 59 us -> 4.77 us  [nt(): lax.dot_general(a, b, (((1,), (1,)), ((), ())), preferred_element_type=F32)]
    pmax x1 -> x0, blocking collectives: 38.2 us -> none  [per_device(): slot_peak = lax.pmax(jnp.max(logits, axis=1), ('req', 'mlp'))]
    all_gather x0 -> x1, local copies, waits for them, and re-layouts: none -> 16.6 us  [body(): weights = lax.all_gather(merged, 'req', axis=0)]
  transfers between devices with their start and end apart: 6 -> 68, of which waited for: 6 -> 26; matrix products, arithmetic and copies ran while one was open for 10% -> 13% of each run, Pallas kernels for 0% -> 20%
where the time goes in v1:
time: 536 us; the launch traced here: 526 us
  waiting for transfers between devices  167 us (31%)
  starting transfers between devices  148 us (28%)
  Pallas kernels  103 us (19%)
  local copies, waits for them, and re-layouts  53.8 us (10%)
  other arithmetic  31.4 us (6%)
  between operations  19.5 us (4%)
    ppermute x12, starting transfers between devices, reduce_to_owners(): lax.ppermute(message if right is None else message + right, 'mlp', [(i, i...  77.5 us
    ppermute x12, waiting for transfers between devices, spread(): lax.ppermute(lefts[-1], 'mlp', [(i + 1, i) for i in range(0, nz - s)])  74.1 us
    ppermute x12, waiting for transfers between devices, reduce_to_owners(): lax.ppermute(message if right is None else message + right, 'mlp', [(i, i...  52.9 us
    pallas_call x2, Pallas kernels, body(): call(functools.partial(unit_kernel, nz), (weights.shape[2] // unit,), [sp...  29.6 us
    ppermute x12, starting transfers between devices, spread(): lax.ppermute(rights[-1], 'mlp', [(i, i + 1) for i in range(s - 1, nz - 1)])  25.8 us
    ppermute x12, waiting for transfers between devices, spread(): lax.ppermute(rights[-1], 'mlp', [(i, i + 1) for i in range(s - 1, nz - 1)])  22.8 us
    unnamed x116, local copies, waits for them, and re-layouts  20.5 us
    pallas_call x1, Pallas kernels, body(): call(project_kernel, (3, blocks), [pl.BlockSpec((block, width), lambda p,...  18.6 us
  transfers between devices with their start and end apart: 68, of which 26 were waited for; matrix products, arithmetic and copies ran while one was open for 13% of the time, Pallas kernels for 20%

profile of v1, /device:TPU:0, one launch (start us, length us, event | category | flops | bytes accessed | tf_op | source)
XLA Modules:
  0.0 526.3 jit_solution(15391782828658101555)
XLA Ops:
  7.2 3.4 fusion.16
  30.0 18.6 %shard_map.184 = (bf16[1024,512]{1,0:T(8,128)(2,1)}, bf16[1024,512]{1,0:T(8,128)(2,1)}, f32[1024,512]{1,0:T(8,128)}, bf16[1024,2048]{1,0:T(8,128)(2,1)}) custom-call(s32[28]{0:T(128)} %concatenate.15.info, bf16[1024,2048]{1,0:T(8,128)(2,1)} %bitcast.116, f32[1,2048]{1,0:T(1,128)} %bitcast.118, bf16[3,2048,512]{2,1,0:T(8,128)(2,1)} %bitcast.115, ...), custom_call_target="tpu_custom_call" | custom-call | flops 6442450944 | bytes 14680064 | tf_op jit(solution)/shard_map/pallas_call | solution.py:354
  49.9 17.4 %shard_map.186.own_ref = bf16[1024,512]{1,0:T(8,128)(2,1)} custom-call(s32[28]{0:T(128)} %concatenate.15.info, f32[1024,512]{1,0:T(8,128)} %get-tuple-element.27.q_ref, bf16[1024,512]{1,0:T(8,128)(2,1)} %get-tuple-element.28.k_ref, bf16[1024,512]{1,0:T(8,128)(2,1)} %get-tuple-element.29.v_ref, bf16[1024,2048]{1,0:T(8,128)(2,1)} %get-tuple-element.30.normed_ref, ...), custom_call_target="tpu_custom_call" | custom-call | flops 2147483648 | bytes 9437184 | tf_op jit(solution)/shard_map/pallas_call | solution.py:385
  72.2 6.9 %shard_map.187.part_ref = bf16[4,144,2048]{2,1,0:T(8,128)(2,1)} custom-call(s32[28]{0:T(128)} %concatenate.15.info, bf16[1024,512]{1,0:T(8,128)(2,1)} %shard_map.186.own_ref, bf16[1024,512]{1,0:T(8,128)(2,1)} %copy-done.37, bf16[512,2048]{1,0:T(8,128)(2,1)} %w_ref.3), custom_call_target="tpu_custom_call" | custom-call | flops 2415919104 | bytes 6553600 | tf_op jit(solution)/shard_map/pallas_call | solution.py:421
  83.0 3.6 collective-permute-start.8
  90.2 9.4 %collective-permute-done.8 = bf16[144,2048]{1,0:T(8,128)(2,1)S(1)} collective-permute-done((bf16[144,2048]{1,0:T(8,128)(2,1)S(1)}, bf16[144,2048]{1,0:T(8,128)(2,1)S(1)}, u32[]{:S(2)}, u32[]{:S(2)}) %collective-permute-start.8) | collective-permute-done | bytes 589856 | tf_op jit(solution)/shard_map/ppermute | solution.py:297
  102.6 22.4 %collective-permute-start.9 = (bf16[144,2048]{1,0:T(8,128)(2,1)}, bf16[144,2048]{1,0:T(8,128)(2,1)}, u32[]{:S(2)}, u32[]{:S(2)}) collective-permute-start(bf16[144,2048]{1,0:T(8,128)(2,1)} %get-tuple-element.68), channel_id=1, source_target_pairs={{0,1},{1,2},{4,5},{5,6},{8,9},{9,10},{12,13},{13,14},{16,17},{17,1... | collective-permute-start | bytes 1769480 | tf_op jit(solution)/shard_map/ppermute | solution.py:297
  125.1 6.2 %shard_map.188 = (bf16[144,2048]{1,0:T(8,128)(2,1)}, bf16[128,2048]{1,0:T(8,128)(2,1)}, bf16[144,2048]{1,0:T(8,128)(2,1)}, bf16[128,2048]{1,0:T(8,128)(2,1)}) custom-call(s32[28]{0:T(128)} %concatenate.15.info, bf16[1024,2048]{1,0:T(8,128)(2,1)} %bitcast.117), custom_call_target="tpu_custom_call" | custom-call | flops 2281701376 | bytes 4194304 | tf_op jit(solution)/shard_map/pallas_call | solution.py:402
  131.3 6.6 %shard_map.192.part_ref = bf16[4,128,2048]{2,1,0:T(8,128)(2,1)} custom-call(s32[28]{0:T(128)} %concatenate.15.info, bf16[1024,512]{1,0:T(8,128)(2,1)} %shard_map.186.own_ref, bf16[1024,512]{1,0:T(8,128)(2,1)} %copy-done.37, bf16[512,2048]{1,0:T(8,128)(2,1)} %w_ref.3), custom_call_target="tpu_custom_call" | custom-call | flops 2147483648 | bytes 6291456 | tf_op jit(solution)/shard_map/pallas_call | solution.py:421
  140.3 4.7 collective-permute-start.10
  149.9 5.6 %collective-permute-done.13.left = bf16[144,2048]{1,0:T(8,128)(2,1)S(1)} collective-permute-done((bf16[144,2048]{1,0:T(8,128)(2,1)S(1)}, bf16[144,2048]{1,0:T(8,128)(2,1)S(1)}, u32[]{:S(2)}, u32[]{:S(2)}) %collective-permute-start.13) | collective-permute-done | bytes 589856 | tf_op jit(solution)/shard_map/ppermute | solution.py:301
  155.5 3.2 collective-permute-done.10.right
  159.5 4.0 shard_map.189
  163.5 4.4 collective-permute-start.15
  170.0 11.9 %collective-permute-done.15.rest_0_ = bf16[144,2048]{1,0:T(8,128)(2,1)S(1)} collective-permute-done((bf16[144,2048]{1,0:T(8,128)(2,1)}, bf16[144,2048]{1,0:T(8,128)(2,1)S(1)}, u32[]{:S(2)}, u32[]{:S(2)}) %collective-permute-start.15) | collective-permute-done | bytes 589856 | tf_op jit(solution)/shard_map/ppermute | solution.py:312
  185.1 14.7 %collective-permute-start.35 = (bf16[128,2048]{1,0:T(8,128)(2,1)S(1)}, bf16[128,2048]{1,0:T(8,128)(2,1)S(1)}, u32[]{:S(2)}, u32[]{:S(2)}) collective-permute-start(bf16[128,2048]{1,0:T(8,128)(2,1)S(1)} %get-tuple-element.76), channel_id=1, source_target_pairs={{0,1},{1,2},{4,5},{5,6},{8,9},{9,10},{12,13},{13,14},{16,17},{17,1... | collective-permute-start | bytes 1572872 | tf_op jit(solution)/shard_map/ppermute | solution.py:297
  203.2 4.2 collective-permute-done.35
  207.5 6.4 %collective-permute-start.36 = (bf16[128,2048]{1,0:T(8,128)(2,1)S(1)}, bf16[128,2048]{1,0:T(8,128)(2,1)S(1)}, u32[]{:S(2)}, u32[]{:S(2)}) collective-permute-start(bf16[128,2048]{1,0:T(8,128)(2,1)S(1)} %bitcast_add_fusion.15), channel_id=1, source_target_pairs={{0,1},{1,2},{2,3},{4,5},{5,6},{6,7},{8,9},{9,10},{10,11},{12,13},{... | collective-permute-start | bytes 1572872 | tf_op jit(solution)/shard_map/ppermute | solution.py:297
  216.5 4.9 collective-permute-done.36.right
  222.2 3.7 shard_map.193
  225.9 4.4 collective-permute-start.41
  231.9 16.6 %copy.25 = bf16[6144,1024]{1,0:T(8,128)(2,1)} copy(bf16[6144,1024]{0,1:T(8,128)(2,1)} %all-gather.3.cloned.1.call-done) | data formatting | bytes 25165824 | tf_op jit(solution)/shard_map/all_gather | solution.py:335
  249.5 15.4 %shard_map.190.part_ref = bf16[4,144,2048]{2,1,0:T(8,128)(2,1)} custom-call(s32[28]{0:T(128)} %concatenate.15.info, bf16[144,2048]{1,0:T(8,128)(2,1)} %get-tuple-element.41.own, bf16[144,2048]{1,0:T(8,128)(2,1)} %copy-done.38, bf16[144,2048]{1,0:T(8,128)(2,1)} %copy-done.40, bf16[144,2048]{1,0:T(8,128)(2,1)} %copy-done.41, bf16[144,2048]{1,0:T(8,128)(2,1)} %copy-done.39, ...), custom_call_target="tpu_custom_call" | custom-call | flops 7247757312 | bytes 12582912 | tf_op jit(solution)/shard_map/pallas_call | solution.py:441
  269.8 21.7 %collective-permute-done.45.rest_4_ = bf16[128,2048]{1,0:T(8,128)(2,1)S(1)} collective-permute-done((bf16[128,2048]{1,0:T(8,128)(2,1)S(1)}, bf16[128,2048]{1,0:T(8,128)(2,1)S(1)}, u32[]{:S(2)}, u32[]{:S(2)}) %collective-permute-start.45) | collective-permute-done | bytes 524320 | tf_op jit(solution)/shard_map/ppermute | solution.py:313
  292.7 4.6 collective-permute-start.21
  299.4 6.3 %collective-permute-done.46.rest_5_ = bf16[128,2048]{1,0:T(8,128)(2,1)S(1)} collective-permute-done((bf16[128,2048]{1,0:T(8,128)(2,1)S(1)}, bf16[128,2048]{1,0:T(8,128)(2,1)S(1)}, u32[]{:S(2)}, u32[]{:S(2)}) %collective-permute-start.46) | collective-permute-done | bytes 524320 | tf_op jit(solution)/shard_map/ppermute | solution.py:313
  306.5 14.2 %shard_map.194.part_ref = bf16[4,128,2048]{2,1,0:T(8,128)(2,1)} custom-call(s32[28]{0:T(128)} %concatenate.15.info, bf16[128,2048]{1,0:T(8,128)(2,1)} %get-tuple-element.46.own, bf16[128,2048]{1,0:T(8,128)(2,1)} %copy-done.44, bf16[128,2048]{1,0:T(8,128)(2,1)} %copy-done.46, bf16[128,2048]{1,0:T(8,128)(2,1)} %copy-done.48, bf16[128,2048]{1,0:T(8,128)(2,1)} %copy-done.45, ...), custom_call_target="tpu_custom_call" | custom-call | flops 6442450944 | bytes 12582912 | tf_op jit(solution)/shard_map/pallas_call | solution.py:441
  324.4 3.4 collective-permute-start.47
  329.9 8.2 %collective-permute-done.22 = bf16[144,2048]{1,0:T(8,128)(2,1)S(1)} collective-permute-done((bf16[144,2048]{1,0:T(8,128)(2,1)S(1)}, bf16[144,2048]{1,0:T(8,128)(2,1)S(1)}, u32[]{:S(2)}, u32[]{:S(2)}) %collective-permute-start.22) | collective-permute-done | bytes 589856 | tf_op jit(solution)/shard_map/ppermute | solution.py:297
  338.2 4.4 collective-permute-start.23
  342.6 6.7 %collective-permute-done.47 = bf16[128,2048]{1,0:T(8,128)(2,1)S(1)} collective-permute-done((bf16[128,2048]{1,0:T(8,128)(2,1)S(1)}, bf16[128,2048]{1,0:T(8,128)(2,1)S(1)}, u32[]{:S(2)}, u32[]{:S(2)}) %collective-permute-start.47) | collective-permute-done | bytes 524320 | tf_op jit(solution)/shard_map/ppermute | solution.py:297
  349.5 4.4 collective-permute-start.48
  355.3 6.7 %collective-permute-done.23.right = bf16[144,2048]{1,0:T(8,128)(2,1)S(1)} collective-permute-done((bf16[144,2048]{1,0:T(8,128)(2,1)S(1)}, bf16[144,2048]{1,0:T(8,128)(2,1)S(1)}, u32[]{:S(2)}, u32[]{:S(2)}) %collective-permute-start.23) | collective-permute-done | bytes 589856 | tf_op jit(solution)/shard_map/ppermute | solution.py:297
  362.9 3.5 shard_map.191
  366.4 4.4 collective-permute-start.27
  373.3 4.5 collective-permute-start.49
  379.2 6.8 %collective-permute-done.27 = bf16[144,2048]{1,0:T(8,128)(2,1)S(1)} collective-permute-done((bf16[144,2048]{1,0:T(8,128)(2,1)}, bf16[144,2048]{1,0:T(8,128)(2,1)S(1)}, u32[]{:S(2)}, u32[]{:S(2)}) %collective-permute-start.27) | collective-permute-done | bytes 589856 | tf_op jit(solution)/shard_map/ppermute | solution.py:312
  386.7 7.1 %collective-permute-done.49.right = bf16[128,2048]{1,0:T(8,128)(2,1)S(1)} collective-permute-done((bf16[128,2048]{1,0:T(8,128)(2,1)S(1)}, bf16[128,2048]{1,0:T(8,128)(2,1)S(1)}, u32[]{:S(2)}, u32[]{:S(2)}) %collective-permute-start.49) | collective-permute-done | bytes 524320 | tf_op jit(solution)/shard_map/ppermute | solution.py:297
  394.6 3.4 shard_map.195
  398.0 5.2 collective-permute-start.53
  406.8 4.0 collective-permute-done.53
  412.3 15.9 %collective-permute-done.56 = bf16[128,2048]{1,0:T(8,128)(2,1)} collective-permute-done((bf16[128,2048]{1,0:T(8,128)(2,1)}, bf16[128,2048]{1,0:T(8,128)(2,1)}, u32[]{:S(2)}, u32[]{:S(2)}) %collective-permute-start.56) | collective-permute-done | bytes 524320 | tf_op jit(solution)/shard_map/ppermute | solution.py:313
  432.6 19.7 %collective-permute-done.32 = bf16[144,2048]{1,0:T(8,128)(2,1)S(1)} collective-permute-done((bf16[144,2048]{1,0:T(8,128)(2,1)S(1)}, bf16[144,2048]{1,0:T(8,128)(2,1)S(1)}, u32[]{:S(2)}, u32[]{:S(2)}) %collective-permute-start.32) | collective-permute-done | bytes 589856 | tf_op jit(solution)/shard_map/ppermute | solution.py:313
  467.2 9.3 %collective-permute-done.58 = bf16[128,2048]{1,0:T(8,128)(2,1)S(1)} collective-permute-done((bf16[128,2048]{1,0:T(8,128)(2,1)}, bf16[128,2048]{1,0:T(8,128)(2,1)S(1)}, u32[]{:S(2)}, u32[]{:S(2)}) %collective-permute-start.58) | collective-permute-done | bytes 524320 | tf_op jit(solution)/shard_map/ppermute | solution.py:313
  489.7 4.0 select_dynamic-update-slice_fusion
  493.7 4.8 convolution_reduce_fusion
  502.6 3.7 select_dynamic-update-slice_fusion.1
  510.1 3.7 select_bitcast_fusion.1
  (285 shorter events, 127.3 us)
Async XLA Ops:
  7.2 224.7 %all-gather.3.cloned.1.call-start = ((), (), s32[]{:S(2)}) async-start(), calls=%async_computation | async-start | bytes 14155776 | tf_op jit(solution)/shard_map/all_gather | solution.py:335
  22.4 26.2 %collective-permute-start.2 = (bf16[2,16,2560]{2,1,0:T(8,128)(2,1)}, bf16[2,16,2560]{2,1,0:T(8,128)(2,1)S(1)}, u32[]{:S(2)}, u32[]{:S(2)}) collective-permute-start(bf16[2,16,2560]{2,1,0:T(8,128)(2,1)} %get-tuple-element.34), channel_id=1, source_target_pairs={{0,12},{4,8},{8,4},{12,0},{16,28},{20,24},{24,20},{28,16},{1,13},{... | collective-permute-start | bytes 491528 | tf_op jit(solution)/shard_map/ppermute | solution.py:346
  22.5 26.1 %collective-permute-start.3 = (bf16[2,16,2560]{2,1,0:T(8,128)(2,1)}, bf16[2,16,2560]{2,1,0:T(8,128)(2,1)S(1)}, u32[]{:S(2)}, u32[]{:S(2)}) collective-permute-start(bf16[2,16,2560]{2,1,0:T(8,128)(2,1)} %get-tuple-element.35), channel_id=1, source_target_pairs={{0,16},{4,20},{8,24},{12,28},{16,0},{20,4},{24,8},{28,12},{1,17},{... | collective-permute-start | bytes 491528 | tf_op jit(solution)/shard_map/ppermute | solution.py:346
  24.3 24.4 %collective-permute-start.4 = (bf16[2,16,2560]{2,1,0:T(8,128)(2,1)}, bf16[2,16,2560]{2,1,0:T(8,128)(2,1)S(1)}, u32[]{:S(2)}, u32[]{:S(2)}) collective-permute-start(bf16[2,16,2560]{2,1,0:T(8,128)(2,1)} %get-tuple-element.36), channel_id=1, source_target_pairs={{0,20},{4,16},{8,28},{12,24},{16,4},{20,0},{24,12},{28,8},{1,21},{... | collective-permute-start | bytes 491528 | tf_op jit(solution)/shard_map/ppermute | solution.py:346
  24.3 24.4 %collective-permute-start.5 = (bf16[2,16,2560]{2,1,0:T(8,128)(2,1)}, bf16[2,16,2560]{2,1,0:T(8,128)(2,1)S(1)}, u32[]{:S(2)}, u32[]{:S(2)}) collective-permute-start(bf16[2,16,2560]{2,1,0:T(8,128)(2,1)} %get-tuple-element.37), channel_id=1, source_target_pairs={{0,24},{4,28},{8,16},{12,20},{16,8},{20,12},{24,0},{28,4},{1,25},{... | collective-permute-start | bytes 491528 | tf_op jit(solution)/shard_map/ppermute | solution.py:346
  28.6 20.7 %collective-permute-start.6 = (bf16[2,16,2560]{2,1,0:T(8,128)(2,1)}, bf16[2,16,2560]{2,1,0:T(8,128)(2,1)S(1)}, u32[]{:S(2)}, u32[]{:S(2)}) collective-permute-start(bf16[2,16,2560]{2,1,0:T(8,128)(2,1)} %get-tuple-element.38), channel_id=1, source_target_pairs={{0,28},{4,24},{8,20},{12,16},{16,12},{20,8},{24,4},{28,0},{1,29},{... | collective-permute-start | bytes 491528 | tf_op jit(solution)/shard_map/ppermute | solution.py:346
  83.0 16.7 %collective-permute-start.8 = (bf16[144,2048]{1,0:T(8,128)(2,1)S(1)}, bf16[144,2048]{1,0:T(8,128)(2,1)S(1)}, u32[]{:S(2)}, u32[]{:S(2)}) collective-permute-start(bf16[144,2048]{1,0:T(8,128)(2,1)S(1)} %get-tuple-element.70), channel_id=1, source_target_pairs={{0,1},{4,5},{8,9},{12,13},{16,17},{20,21},{24,25},{28,29}} | collective-permute-start | bytes 1769480 | tf_op jit(solution)/shard_map/ppermute | solution.py:297
  102.6 36.5 %collective-permute-start.9 = (bf16[144,2048]{1,0:T(8,128)(2,1)}, bf16[144,2048]{1,0:T(8,128)(2,1)}, u32[]{:S(2)}, u32[]{:S(2)}) collective-permute-start(bf16[144,2048]{1,0:T(8,128)(2,1)} %get-tuple-element.68), channel_id=1, source_target_pairs={{0,1},{1,2},{4,5},{5,6},{8,9},{9,10},{12,13},{13,14},{16,17},{17,1... | collective-permute-start | bytes 1769480 | tf_op jit(solution)/shard_map/ppermute | solution.py:297
  131.3 18.6 %collective-permute-start.14 = (bf16[144,2048]{1,0:T(8,128)(2,1)}, bf16[144,2048]{1,0:T(8,128)(2,1)S(1)}, u32[]{:S(2)}, u32[]{:S(2)}) collective-permute-start(bf16[144,2048]{1,0:T(8,128)(2,1)} %get-tuple-element.40), channel_id=1, source_target_pairs={{0,4},{4,0},{8,12},{12,8},{16,20},{20,16},{24,28},{28,24},{1,5},{5... | collective-permute-start | bytes 1769480 | tf_op jit(solution)/shard_map/ppermute | solution.py:412
  137.9 17.6 %collective-permute-start.13 = (bf16[144,2048]{1,0:T(8,128)(2,1)S(1)}, bf16[144,2048]{1,0:T(8,128)(2,1)S(1)}, u32[]{:S(2)}, u32[]{:S(2)}) collective-permute-start(bf16[144,2048]{1,0:T(8,128)(2,1)S(1)} %get-tuple-element.67), channel_id=1, source_target_pairs={{3,2},{2,1},{1,0},{7,6},{6,5},{5,4},{11,10},{10,9},{9,8},{15,14},{... | collective-permute-start | bytes 1769480 | tf_op jit(solution)/shard_map/ppermute | solution.py:301
  140.3 18.3 %collective-permute-start.10 = (bf16[144,2048]{1,0:T(8,128)(2,1)S(1)}, bf16[144,2048]{1,0:T(8,128)(2,1)S(1)}, u32[]{:S(2)}, u32[]{:S(2)}) collective-permute-start(bf16[144,2048]{1,0:T(8,128)(2,1)S(1)} %bitcast_add_fusion.7), channel_id=1, source_target_pairs={{0,1},{1,2},{2,3},{4,5},{5,6},{6,7},{8,9},{9,10},{10,11},{12,13},{... | collective-permute-start | bytes 1769480 | tf_op jit(solution)/shard_map/ppermute | solution.py:297
  146.4 22.9 %collective-permute-start.37 = (bf16[128,2048]{1,0:T(8,128)(2,1)S(1)}, bf16[128,2048]{1,0:T(8,128)(2,1)S(1)}, u32[]{:S(2)}, u32[]{:S(2)}) collective-permute-start(bf16[128,2048]{1,0:T(8,128)(2,1)S(1)} %get-tuple-element.77), channel_id=1, source_target_pairs={{3,2},{7,6},{11,10},{15,14},{19,18},{23,22},{27,26},{31,30}} | collective-permute-start | bytes 1572872 | tf_op jit(solution)/shard_map/ppermute | solution.py:301
  147.1 38.0 %collective-permute-start.34 = (bf16[128,2048]{1,0:T(8,128)(2,1)S(1)}, bf16[128,2048]{1,0:T(8,128)(2,1)S(1)}, u32[]{:S(2)}, u32[]{:S(2)}) collective-permute-start(bf16[128,2048]{1,0:T(8,128)(2,1)S(1)} %get-tuple-element.78), channel_id=1, source_target_pairs={{0,1},{4,5},{8,9},{12,13},{16,17},{20,21},{24,25},{28,29}} | collective-permute-start | bytes 1572872 | tf_op jit(solution)/shard_map/ppermute | solution.py:297
  163.5 18.4 %collective-permute-start.15 = (bf16[144,2048]{1,0:T(8,128)(2,1)}, bf16[144,2048]{1,0:T(8,128)(2,1)S(1)}, u32[]{:S(2)}, u32[]{:S(2)}) collective-permute-start(bf16[144,2048]{1,0:T(8,128)(2,1)} %get-tuple-element.41.own), channel_id=1, source_target_pairs={{0,1},{1,2},{2,3},{4,5},{5,6},{6,7},{8,9},{9,10},{10,11},{12,13},{... | collective-permute-start | bytes 1769480 | tf_op jit(solution)/shard_map/ppermute | solution.py:312
  167.9 15.8 %collective-permute-start.18 = (bf16[144,2048]{1,0:T(8,128)(2,1)}, bf16[144,2048]{1,0:T(8,128)(2,1)S(1)}, u32[]{:S(2)}, u32[]{:S(2)}) collective-permute-start(bf16[144,2048]{1,0:T(8,128)(2,1)} %get-tuple-element.41.own), channel_id=1, source_target_pairs={{1,0},{2,1},{3,2},{5,4},{6,5},{7,6},{9,8},{10,9},{11,10},{13,12},{... | collective-permute-start | bytes 1769480 | tf_op jit(solution)/shard_map/ppermute | solution.py:313
  182.0 19.2 %collective-permute-start.16 = (bf16[144,2048]{1,0:T(8,128)(2,1)S(1)}, bf16[144,2048]{1,0:T(8,128)(2,1)S(1)}, u32[]{:S(2)}, u32[]{:S(2)}) collective-permute-start(bf16[144,2048]{1,0:T(8,128)(2,1)S(1)} %collective-permute-done.15.rest_0_), channel_id=1, source_target_pairs={{1,2},{2,3},{5,6},{6,7},{9,10},{10,11},{13,14},{14,15},{17,18},{18... | collective-permute-start | bytes 1769480 | tf_op jit(solution)/shard_map/ppermute | solution.py:312
  183.7 18.2 %collective-permute-start.19 = (bf16[144,2048]{1,0:T(8,128)(2,1)S(1)}, bf16[144,2048]{1,0:T(8,128)(2,1)}, u32[]{:S(2)}, u32[]{:S(2)}) collective-permute-start(bf16[144,2048]{1,0:T(8,128)(2,1)S(1)} %collective-permute-done.18.rest_3_), channel_id=1, source_target_pairs={{1,0},{2,1},{5,4},{6,5},{9,8},{10,9},{13,12},{14,13},{17,16},{18,1... | collective-permute-start | bytes 1769480 | tf_op jit(solution)/shard_map/ppermute | solution.py:313
  185.1 22.3 %collective-permute-start.35 = (bf16[128,2048]{1,0:T(8,128)(2,1)S(1)}, bf16[128,2048]{1,0:T(8,128)(2,1)S(1)}, u32[]{:S(2)}, u32[]{:S(2)}) collective-permute-start(bf16[128,2048]{1,0:T(8,128)(2,1)S(1)} %get-tuple-element.76), channel_id=1, source_target_pairs={{0,1},{1,2},{4,5},{5,6},{8,9},{9,10},{12,13},{13,14},{16,17},{17,1... | collective-permute-start | bytes 1572872 | tf_op jit(solution)/shard_map/ppermute | solution.py:297
  199.9 16.6 %collective-permute-start.39 = (bf16[128,2048]{1,0:T(8,128)(2,1)S(1)}, bf16[128,2048]{1,0:T(8,128)(2,1)S(1)}, u32[]{:S(2)}, u32[]{:S(2)}) collective-permute-start(bf16[128,2048]{1,0:T(8,128)(2,1)S(1)} %get-tuple-element.75), channel_id=1, source_target_pairs={{3,2},{2,1},{1,0},{7,6},{6,5},{5,4},{11,10},{10,9},{9,8},{15,14},{... | collective-permute-start | bytes 1572872 | tf_op jit(solution)/shard_map/ppermute | solution.py:301
  201.2 47.3 %collective-permute-start.17 = (bf16[144,2048]{1,0:T(8,128)(2,1)S(1)}, bf16[144,2048]{1,0:T(8,128)(2,1)S(1)}, u32[]{:S(2)}, u32[]{:S(2)}) collective-permute-start(bf16[144,2048]{1,0:T(8,128)(2,1)S(1)} %collective-permute-done.16.rest_1_), channel_id=1, source_target_pairs={{2,3},{6,7},{10,11},{14,15},{18,19},{22,23},{26,27},{30,31}} | collective-permute-start | bytes 1769480 | tf_op jit(solution)/shard_map/ppermute | solution.py:312
  201.9 46.6 %collective-permute-start.20 = (bf16[144,2048]{1,0:T(8,128)(2,1)}, bf16[144,2048]{1,0:T(8,128)(2,1)S(1)}, u32[]{:S(2)}, u32[]{:S(2)}) collective-permute-start(bf16[144,2048]{1,0:T(8,128)(2,1)} %collective-permute-done.19.rest_4_), channel_id=1, source_target_pairs={{1,0},{5,4},{9,8},{13,12},{17,16},{21,20},{25,24},{29,28}} | collective-permute-start | bytes 1769480 | tf_op jit(solution)/shard_map/ppermute | solution.py:313
  225.9 41.1 %collective-permute-start.41 = (bf16[128,2048]{1,0:T(8,128)(2,1)}, bf16[128,2048]{1,0:T(8,128)(2,1)S(1)}, u32[]{:S(2)}, u32[]{:S(2)}) collective-permute-start(bf16[128,2048]{1,0:T(8,128)(2,1)} %get-tuple-element.46.own), channel_id=1, source_target_pairs={{0,1},{1,2},{2,3},{4,5},{5,6},{6,7},{8,9},{9,10},{10,11},{12,13},{... | collective-permute-start | bytes 1572872 | tf_op jit(solution)/shard_map/ppermute | solution.py:312
  230.3 37.4 %collective-permute-start.44 = (bf16[128,2048]{1,0:T(8,128)(2,1)}, bf16[128,2048]{1,0:T(8,128)(2,1)S(1)}, u32[]{:S(2)}, u32[]{:S(2)}) collective-permute-start(bf16[128,2048]{1,0:T(8,128)(2,1)} %get-tuple-element.46.own), channel_id=1, source_target_pairs={{1,0},{2,1},{3,2},{5,4},{6,5},{7,6},{9,8},{10,9},{11,10},{13,12},{... | collective-permute-start | bytes 1572872 | tf_op jit(solution)/shard_map/ppermute | solution.py:313
  266.3 31.1 %collective-permute-start.24 = (bf16[144,2048]{1,0:T(8,128)(2,1)S(1)}, bf16[144,2048]{1,0:T(8,128)(2,1)S(1)}, u32[]{:S(2)}, u32[]{:S(2)}) collective-permute-start(bf16[144,2048]{1,0:T(8,128)(2,1)S(1)} %get-tuple-element.65), channel_id=1, source_target_pairs={{3,2},{7,6},{11,10},{15,14},{19,18},{23,22},{27,26},{31,30}} | collective-permute-start | bytes 1769480 | tf_op jit(solution)/shard_map/ppermute | solution.py:301
  267.7 23.7 %collective-permute-start.45 = (bf16[128,2048]{1,0:T(8,128)(2,1)S(1)}, bf16[128,2048]{1,0:T(8,128)(2,1)S(1)}, u32[]{:S(2)}, u32[]{:S(2)}) collective-permute-start(bf16[128,2048]{1,0:T(8,128)(2,1)S(1)} %collective-permute-done.44.rest_3_), channel_id=1, source_target_pairs={{1,0},{2,1},{5,4},{6,5},{9,8},{10,9},{13,12},{14,13},{17,16},{18,1... | collective-permute-start | bytes 1572872 | tf_op jit(solution)/shard_map/ppermute | solution.py:313
  269.1 30.3 %collective-permute-start.43 = (bf16[128,2048]{1,0:T(8,128)(2,1)S(1)}, bf16[128,2048]{1,0:T(8,128)(2,1)S(1)}, u32[]{:S(2)}, u32[]{:S(2)}) collective-permute-start(bf16[128,2048]{1,0:T(8,128)(2,1)S(1)} %collective-permute-done.42.rest_1_), channel_id=1, source_target_pairs={{2,3},{6,7},{10,11},{14,15},{18,19},{22,23},{26,27},{30,31}} | collective-permute-start | bytes 1572872 | tf_op jit(solution)/shard_map/ppermute | solution.py:312
  292.7 30.0 %collective-permute-start.21 = (bf16[144,2048]{1,0:T(8,128)(2,1)S(1)}, bf16[144,2048]{1,0:T(8,128)(2,1)S(1)}, u32[]{:S(2)}, u32[]{:S(2)}) collective-permute-start(bf16[144,2048]{1,0:T(8,128)(2,1)S(1)} %get-tuple-element.66), channel_id=1, source_target_pairs={{0,1},{4,5},{8,9},{12,13},{16,17},{20,21},{24,25},{28,29}} | collective-permute-start | bytes 1769480 | tf_op jit(solution)/shard_map/ppermute | solution.py:297
  298.5 24.3 %collective-permute-start.25 = (bf16[144,2048]{1,0:T(8,128)(2,1)S(1)}, bf16[144,2048]{1,0:T(8,128)(2,1)S(1)}, u32[]{:S(2)}, u32[]{:S(2)}) collective-permute-start(bf16[144,2048]{1,0:T(8,128)(2,1)S(1)} %bitcast_add_fusion), channel_id=1, source_target_pairs={{3,2},{2,1},{7,6},{6,5},{11,10},{10,9},{15,14},{14,13},{19,18},{18... | collective-permute-start | bytes 1769480 | tf_op jit(solution)/shard_map/ppermute | solution.py:301
  324.4 25.0 %collective-permute-start.47 = (bf16[128,2048]{1,0:T(8,128)(2,1)S(1)}, bf16[128,2048]{1,0:T(8,128)(2,1)S(1)}, u32[]{:S(2)}, u32[]{:S(2)}) collective-permute-start(bf16[128,2048]{1,0:T(8,128)(2,1)S(1)} %get-tuple-element.74), channel_id=1, source_target_pairs={{0,1},{4,5},{8,9},{12,13},{16,17},{20,21},{24,25},{28,29}} | collective-permute-start | bytes 1572872 | tf_op jit(solution)/shard_map/ppermute | solution.py:297
  327.9 21.5 %collective-permute-start.51 = (bf16[128,2048]{1,0:T(8,128)(2,1)S(1)}, bf16[128,2048]{1,0:T(8,128)(2,1)S(1)}, u32[]{:S(2)}, u32[]{:S(2)}) collective-permute-start(bf16[128,2048]{1,0:T(8,128)(2,1)S(1)} %bitcast_add_fusion.8), channel_id=1, source_target_pairs={{3,2},{2,1},{7,6},{6,5},{11,10},{10,9},{15,14},{14,13},{19,18},{18... | collective-permute-start | bytes 1572872 | tf_op jit(solution)/shard_map/ppermute | solution.py:301
  328.6 26.6 %collective-permute-start.26 = (bf16[144,2048]{1,0:T(8,128)(2,1)S(1)}, bf16[144,2048]{1,0:T(8,128)(2,1)S(1)}, u32[]{:S(2)}, u32[]{:S(2)}) collective-permute-start(bf16[144,2048]{1,0:T(8,128)(2,1)S(1)} %get-tuple-element.63), channel_id=1, source_target_pairs={{3,2},{2,1},{1,0},{7,6},{6,5},{5,4},{11,10},{10,9},{9,8},{15,14},{... | collective-permute-start | bytes 1769480 | tf_op jit(solution)/shard_map/ppermute | solution.py:301
  338.2 23.8 %collective-permute-start.23 = (bf16[144,2048]{1,0:T(8,128)(2,1)S(1)}, bf16[144,2048]{1,0:T(8,128)(2,1)S(1)}, u32[]{:S(2)}, u32[]{:S(2)}) collective-permute-start(bf16[144,2048]{1,0:T(8,128)(2,1)S(1)} %bitcast_add_fusion.3), channel_id=1, source_target_pairs={{0,1},{1,2},{2,3},{4,5},{5,6},{6,7},{8,9},{9,10},{10,11},{12,13},{... | collective-permute-start | bytes 1769480 | tf_op jit(solution)/shard_map/ppermute | solution.py:297
  349.5 23.7 %collective-permute-start.48 = (bf16[128,2048]{1,0:T(8,128)(2,1)S(1)}, bf16[128,2048]{1,0:T(8,128)(2,1)S(1)}, u32[]{:S(2)}, u32[]{:S(2)}) collective-permute-start(bf16[128,2048]{1,0:T(8,128)(2,1)S(1)} %get-tuple-element.72), channel_id=1, source_target_pairs={{0,1},{1,2},{4,5},{5,6},{8,9},{9,10},{12,13},{13,14},{16,17},{17,1... | collective-permute-start | bytes 1572872 | tf_op jit(solution)/shard_map/ppermute | solution.py:297
  354.0 32.7 %collective-permute-start.52 = (bf16[128,2048]{1,0:T(8,128)(2,1)S(1)}, bf16[128,2048]{1,0:T(8,128)(2,1)S(1)}, u32[]{:S(2)}, u32[]{:S(2)}) collective-permute-start(bf16[128,2048]{1,0:T(8,128)(2,1)S(1)} %get-tuple-element.71), channel_id=1, source_target_pairs={{3,2},{2,1},{1,0},{7,6},{6,5},{5,4},{11,10},{10,9},{9,8},{15,14},{... | collective-permute-start | bytes 1572872 | tf_op jit(solution)/shard_map/ppermute | solution.py:301
  366.4 19.6 %collective-permute-start.27 = (bf16[144,2048]{1,0:T(8,128)(2,1)}, bf16[144,2048]{1,0:T(8,128)(2,1)S(1)}, u32[]{:S(2)}, u32[]{:S(2)}) collective-permute-start(bf16[144,2048]{1,0:T(8,128)(2,1)} %get-tuple-element.43), channel_id=1, source_target_pairs={{0,1},{1,2},{2,3},{4,5},{5,6},{6,7},{8,9},{9,10},{10,11},{12,13},{... | collective-permute-start | bytes 1769480 | tf_op jit(solution)/shard_map/ppermute | solution.py:312
  373.3 20.5 %collective-permute-start.49 = (bf16[128,2048]{1,0:T(8,128)(2,1)S(1)}, bf16[128,2048]{1,0:T(8,128)(2,1)S(1)}, u32[]{:S(2)}, u32[]{:S(2)}) collective-permute-start(bf16[128,2048]{1,0:T(8,128)(2,1)S(1)} %bitcast_add_fusion.11), channel_id=1, source_target_pairs={{0,1},{1,2},{2,3},{4,5},{5,6},{6,7},{8,9},{9,10},{10,11},{12,13},{... | collective-permute-start | bytes 1572872 | tf_op jit(solution)/shard_map/ppermute | solution.py:297
  377.9 25.3 %collective-permute-start.30 = (bf16[144,2048]{1,0:T(8,128)(2,1)}, bf16[144,2048]{1,0:T(8,128)(2,1)S(1)}, u32[]{:S(2)}, u32[]{:S(2)}) collective-permute-start(bf16[144,2048]{1,0:T(8,128)(2,1)} %get-tuple-element.43), channel_id=1, source_target_pairs={{1,0},{2,1},{3,2},{5,4},{6,5},{7,6},{9,8},{10,9},{11,10},{13,12},{... | collective-permute-start | bytes 1769480 | tf_op jit(solution)/shard_map/ppermute | solution.py:313
  386.0 18.5 %collective-permute-start.28 = (bf16[144,2048]{1,0:T(8,128)(2,1)S(1)}, bf16[144,2048]{1,0:T(8,128)(2,1)S(1)}, u32[]{:S(2)}, u32[]{:S(2)}) collective-permute-start(bf16[144,2048]{1,0:T(8,128)(2,1)S(1)} %collective-permute-done.27), channel_id=1, source_target_pairs={{1,2},{2,3},{5,6},{6,7},{9,10},{10,11},{13,14},{14,15},{17,18},{18... | collective-permute-start | bytes 1769480 | tf_op jit(solution)/shard_map/ppermute | solution.py:312
  403.2 27.7 %collective-permute-start.31 = (bf16[144,2048]{1,0:T(8,128)(2,1)S(1)}, bf16[144,2048]{1,0:T(8,128)(2,1)S(1)}, u32[]{:S(2)}, u32[]{:S(2)}) collective-permute-start(bf16[144,2048]{1,0:T(8,128)(2,1)S(1)} %collective-permute-done.30), channel_id=1, source_target_pairs={{1,0},{2,1},{5,4},{6,5},{9,8},{10,9},{13,12},{14,13},{17,16},{18,1... | collective-permute-start | bytes 1769480 | tf_op jit(solution)/shard_map/ppermute | solution.py:313
  404.5 27.7 %collective-permute-start.29 = (bf16[144,2048]{1,0:T(8,128)(2,1)S(1)}, bf16[144,2048]{1,0:T(8,128)(2,1)S(1)}, u32[]{:S(2)}, u32[]{:S(2)}) collective-permute-start(bf16[144,2048]{1,0:T(8,128)(2,1)S(1)} %collective-permute-done.28), channel_id=1, source_target_pairs={{2,3},{6,7},{10,11},{14,15},{18,19},{22,23},{26,27},{30,31}} | collective-permute-start | bytes 1769480 | tf_op jit(solution)/shard_map/ppermute | solution.py:312
  405.5 22.7 %collective-permute-start.56 = (bf16[128,2048]{1,0:T(8,128)(2,1)}, bf16[128,2048]{1,0:T(8,128)(2,1)}, u32[]{:S(2)}, u32[]{:S(2)}) collective-permute-start(bf16[128,2048]{1,0:T(8,128)(2,1)} %get-tuple-element.48), channel_id=1, source_target_pairs={{1,0},{2,1},{3,2},{5,4},{6,5},{7,6},{9,8},{10,9},{11,10},{13,12},{... | collective-permute-start | bytes 1572872 | tf_op jit(solution)/shard_map/ppermute | solution.py:313
  410.8 18.7 %collective-permute-start.54 = (bf16[128,2048]{1,0:T(8,128)(2,1)}, bf16[128,2048]{1,0:T(8,128)(2,1)}, u32[]{:S(2)}, u32[]{:S(2)}) collective-permute-start(bf16[128,2048]{1,0:T(8,128)(2,1)} %collective-permute-done.53), channel_id=1, source_target_pairs={{1,2},{2,3},{5,6},{6,7},{9,10},{10,11},{13,14},{14,15},{17,18},{18... | collective-permute-start | bytes 1572872 | tf_op jit(solution)/shard_map/ppermute | solution.py:312
  428.2 32.0 %collective-permute-start.57 = (bf16[128,2048]{1,0:T(8,128)(2,1)}, bf16[128,2048]{1,0:T(8,128)(2,1)}, u32[]{:S(2)}, u32[]{:S(2)}) collective-permute-start(bf16[128,2048]{1,0:T(8,128)(2,1)} %collective-permute-done.56), channel_id=1, source_target_pairs={{1,0},{2,1},{5,4},{6,5},{9,8},{10,9},{13,12},{14,13},{17,16},{18,1... | collective-permute-start | bytes 1572872 | tf_op jit(solution)/shard_map/ppermute | solution.py:313
  429.5 32.0 %collective-permute-start.55 = (bf16[128,2048]{1,0:T(8,128)(2,1)}, bf16[128,2048]{1,0:T(8,128)(2,1)}, u32[]{:S(2)}, u32[]{:S(2)}) collective-permute-start(bf16[128,2048]{1,0:T(8,128)(2,1)} %collective-permute-done.54), channel_id=1, source_target_pairs={{2,3},{6,7},{10,11},{14,15},{18,19},{22,23},{26,27},{30,31}} | collective-permute-start | bytes 1572872 | tf_op jit(solution)/shard_map/ppermute | solution.py:312
  430.9 21.4 %collective-permute-start.32 = (bf16[144,2048]{1,0:T(8,128)(2,1)S(1)}, bf16[144,2048]{1,0:T(8,128)(2,1)S(1)}, u32[]{:S(2)}, u32[]{:S(2)}) collective-permute-start(bf16[144,2048]{1,0:T(8,128)(2,1)S(1)} %collective-permute-done.31), channel_id=1, source_target_pairs={{1,0},{5,4},{9,8},{13,12},{17,16},{21,20},{25,24},{29,28}} | collective-permute-start | bytes 1769480 | tf_op jit(solution)/shard_map/ppermute | solution.py:313
  455.9 24.0 %collective-permute-start.33 = (bf16[576,2048]{1,0:T(8,128)(2,1)}, bf16[576,2048]{1,0:T(8,128)(2,1)S(1)}, u32[]{:S(2)}, u32[]{:S(2)}) collective-permute-start(bf16[576,2048]{1,0:T(8,128)(2,1)} %constant_dynamic-slice_fusion.2), channel_id=1, source_target_pairs={{0,4},{4,0},{8,12},{12,8},{16,20},{20,16},{24,28},{28,24},{1,5},{5... | collective-permute-start | bytes 7077896 | tf_op jit(solution)/shard_map/ppermute | solution.py:465
  460.2 16.4 %collective-permute-start.58 = (bf16[128,2048]{1,0:T(8,128)(2,1)}, bf16[128,2048]{1,0:T(8,128)(2,1)S(1)}, u32[]{:S(2)}, u32[]{:S(2)}) collective-permute-start(bf16[128,2048]{1,0:T(8,128)(2,1)} %collective-permute-done.57), channel_id=1, source_target_pairs={{1,0},{5,4},{9,8},{13,12},{17,16},{21,20},{25,24},{29,28}} | collective-permute-start | bytes 1572872 | tf_op jit(solution)/shard_map/ppermute | solution.py:313
  479.9 18.7 %collective-permute-start.59 = (bf16[512,2048]{1,0:T(8,128)(2,1)}, bf16[512,2048]{1,0:T(8,128)(2,1)}, u32[]{:S(2)}, u32[]{:S(2)}) collective-permute-start(bf16[512,2048]{1,0:T(8,128)(2,1)} %constant_dynamic-slice_fusion.1), channel_id=1, source_target_pairs={{0,4},{4,0},{8,12},{12,8},{16,20},{20,16},{24,28},{28,24},{1,5},{5... | collective-permute-start | bytes 6291464 | tf_op jit(solution)/shard_map/ppermute | solution.py:465
  (71 other events, 786.5 us)
Sparse Core Ops, SparseCore 0:
  13.9 87.3 all-gather.2
